TPU v7x, 128 devices: a whole 4x4x4 slice. The times are simulated.
128 devices in a mesh: ma: 4 (over y), af: 32 (over x, z, core).
Axes of the slice: x: 4, y: 4, z: 4, core: 2. Of those that a mesh axis runs over, the one named last changes fastest.
Arguments:
- beams: bfloat16 [4, 32, 4, 512, 2048], P(None, 'af', 'ma'), may hold values from -2 to 2
- spectrum: float32 [128, 3, 1024], P('af'), may hold values from 0.3 to 3
- partners: int32 [128, 3], P('af'), may hold values from 0 to 127, as said below
Outputs:
- covariance: bfloat16 [4, 128, 3, 2, 512, 512], P('ma', 'af')
Inputs may be any that keep to these rules, and one draw needn't show every extreme that they name: partners[c, k] lies in the band of c (channels 64 * (c // 64) up to the band's end or the last channel) and at most 2 channels from c; the distance 2 occurs.
All inputs are finite; a program needn't handle non-finite values.
Results may differ from a plain program's by a relative error of at most 0.0044.
Values may be sent and summed in bfloat16 or wider, within the bound.
No kernel may reach another device: no remote copies, remote signals or barrier semaphores. Data moves between devices by JAX's collectives and lax.ppermute only.
A program may use at most 192 MiB of HBM per device.

v0:
```python
import functools

import jax
import jax.numpy as jnp
from jax import lax
from jax.experimental import pallas as pl
from jax.experimental.pallas import tpu as pltpu
from jax.sharding import PartitionSpec as P

BAND = 64
HALF = 256
LATE = 2
VMEM = 56 * 2**20
STAGE_VMEM = 47 * 2**20
CAPS = (9, 10)
FIRST_ROWS = 256
NEAR = 128
WEIGHTS = (10**12, 10**12, 0, 0)
NT = (((1,), (1,)), ((), ()))
ORDER = lax.optimization_barrier


def plan_kernel(stages, caps, partners, *refs):
    lists, loads = refs[:stages], refs[stages]
    chans, slots = partners.shape
    last = 2 * chans * slots
    pos = lax.axis_index("ma")
    group = lax.axis_index("af")
    for stage in range(stages):
        lists[stage][last, 0] = 0
        loads[stage] = 0

    def put(when, stage, kind, half, channel, slot, own, source):
        @pl.when(when)
        def _():
            jobs = lists[stage - 1]
            count = jobs[last, 0]
            own_part = 1 << half if kind == 0 else 3
            source_part = 1 << half if kind == 1 else 3
            mask = jnp.left_shift(own_part, own * 2) | jnp.left_shift(source_part, source * 2)
            for place, field in enumerate((kind, half, channel, slot, own, source, mask)):
                jobs[count, place] = field
            jobs[last, 0] = count + 1
            loads[stage - 1] = loads[stage - 1] + (2 if kind == 2 else 1)

    def visit(late):
        def one(index, carry):
            channel = lax.div(index, slots)
            slot = lax.rem(index, slots)
            offset = partners[channel, slot] - group * chans
            own = lax.rem(channel - pos + 4, 4)
            partner = lax.rem(offset - pos + 8, 4)
            outside = jnp.logical_or(offset < 0, offset >= chans)
            inside = jnp.logical_not(outside)
            source = jnp.where(outside, partner + 4, partner)
            own_late, own_early = own == LATE, own != LATE
            other_late, other_early = partner == LATE, partner != LATE
            early = jnp.logical_or(inside, partner == 0)
            plain = own_early & other_early
            names = dict(channel=channel, slot=slot, own=own, source=source)
            if late:
                put(own_late & other_early, 2, 0, 0, **names)
                put(own_early & other_late & inside, 2, 1, 0, **names)
                put(own_late & other_early, 3, 0, 1, **names)
                put(own_late & other_late & inside, 3, 2, 0, **names)
                put(own_early & other_late & inside, 3, 1, 1, **names)
                put(own_early & other_late & outside, 3, 1, 0, **names)
                put(own_early & other_late & outside, 4, 1, 1, **names)
            else:
                left = plain
                for stage, may in ((1, early), (2, True)):
                    fits = jnp.logical_and(loads[stage - 1] < caps[stage - 1], may)
                    put(left & fits, stage, 2, 0, **names)
                    left = left & jnp.logical_not(fits)
                put(left, 3, 2, 0, **names)
            return carry

        lax.fori_loop(0, chans * slots, one, 0)

    visit(True)
    visit(False)


def make_plan(partners, caps):
    chans, slots = partners.shape
    stages = 4
    scalars = pl.BlockSpec(memory_space=pltpu.SMEM)
    return pl.pallas_call(
        functools.partial(plan_kernel, stages, caps),
        out_shape=[jax.ShapeDtypeStruct((2 * chans * slots + 1, 7), jnp.int32)] * stages,
        in_specs=[scalars],
        out_specs=[scalars] * stages,
        scratch_shapes=[pltpu.SMEM((stages,), jnp.int32)],
        cost_estimate=pl.CostEstimate(flops=10**12, bytes_accessed=1, transcendentals=0),
        name="plan",
    )(partners)


def kernel(kinds, names, ready, fill, keep, *refs):
    jobs, spectrum = refs[:2]
    pieces = dict(zip(names, refs[2 : 2 + len(names)]))
    out, held, state, rows_out, columns_out, whole_out, in_sems, out_sems = refs[-8:]
    outs = (rows_out, columns_out, whole_out)
    pos = lax.axis_index("ma")
    total = jobs[jobs.shape[0] - 1, 0]

    places = {}
    for (source, first), ref in pieces.items():
        if source == 0:
            ref = ref.at[pos]
        for half in range(2):
            low, high = max(first, half * HALF), min(first + ref.shape[0], half * HALF + HALF)
            if low < high and source * 2 + half in fill:
                into = held.at[source * 2 + half, pl.ds(low - half * HALF, high - low)]
                places.setdefault(source * 2 + half, []).append((ref.at[pl.ds(low - first, high - low)], into))
    fresh = sum(1 << part for part in places)
    state[0] = ready
    state[1] = ready

    def each(mask, act):
        @pl.when(mask != 0)
        def _():
            for part, copies in places.items():

                @pl.when(jnp.bitwise_and(mask, 1 << part) != 0)
                def _():
                    for copy in copies:
                        act(pltpu.make_async_copy(*copy, in_sems.at[part]))

    def fetch(wanted):
        mask = wanted & ~state[0]
        each(mask, lambda copy: copy.start())
        state[0] = state[0] | mask

    def arrive(wanted):
        mask = wanted & ~state[1]
        each(mask, lambda copy: copy.wait())
        state[1] = state[1] | mask

    def scaled(block, weights):
        block = block.astype(jnp.float32)
        width = weights.shape[-1]
        real = (block[:, :width] * weights).astype(jnp.bfloat16)
        imag = (block[:, width:] * weights).astype(jnp.bfloat16)
        upper = jnp.concatenate([real, imag], axis=1)
        lower = jnp.concatenate([imag, -real], axis=1)
        return jnp.concatenate([upper, lower], axis=0)

    def write(kind, job, place):
        target = out.at[jobs[job, 2], jobs[job, 3]]
        some = pl.ds(pl.multiple_of(jobs[job, 1] * HALF, HALF), HALF)
        if kind == 0:
            target = target.at[:, some, :]
        if kind == 1:
            target = target.at[:, :, some]
        return pltpu.make_async_copy(outs[kind].at[place], target, out_sems.at[place])

    def drain(job):
        for kind in kinds:

            @pl.when(jobs[job, 0] == kind)
            def _():
                write(kind, job, lax.rem(job, 2)).wait()

    @pl.when(total > 0)
    def _():
        fetch(jobs[0, 6])

    if keep:
        fetch(jnp.int32(fresh))

    def step(job, carry):
        place = lax.rem(job, 2)
        half, own, partner = jobs[job, 1], jobs[job, 4], jobs[job, 5]
        arrive(jobs[job, 6])
        if not keep:

            @pl.when(job + 1 < total)
            def _():
                fetch(jobs[job + 1, 6])

        @pl.when(job >= 2)
        def _():
            drain(job - 2)

        weights = spectrum[jobs[job, 2], pl.ds(jobs[job, 3], 1), :]

        def taken(source, whole):
            if not whole:
                return held[source * 2 + half]
            block = held[pl.ds(source * 2, 2)]
            return block.reshape(2 * HALF, block.shape[2])

        for kind in kinds:

            @pl.when(jobs[job, 0] == kind)
            def _():
                left = scaled(taken(own, kind != 0), weights)
                right = taken(partner, kind != 1)
                product = lax.dot_general(left, right, NT, preferred_element_type=jnp.float32)
                outs[kind][place] = product.astype(jnp.bfloat16).reshape(outs[kind].shape[1:])
                write(kind, job, place).start()

        return carry

    lax.fori_loop(0, total, step, 0)
    if keep:
        arrive(jnp.int32(fresh))

    @pl.when(total >= 2)
    def _():
        drain(total - 2)

    @pl.when(total >= 1)
    def _():
        drain(total - 1)


def run_stage(name, kinds, jobs, spectrum, pieces, ready, fill, held, out, weight):
    chans, slots, _ = spectrum.shape
    names = tuple(pieces)
    arrays = [pieces[name] for name in names]
    rows, width = 2 * HALF, arrays[0].shape[-1]
    whole = pl.BlockSpec(memory_space=pl.ANY)
    vector = pl.BlockSpec(memory_space=pltpu.VMEM)
    operands = [jobs, spectrum, *arrays]
    specs = [pl.BlockSpec(memory_space=pltpu.SMEM), vector] + [whole] * len(arrays)
    aliases = {}
    if out is not None:
        aliases = {len(operands): 0, len(operands) + 1: 1}
        operands += [out, held]
        specs += [whole, vector]
    return pl.pallas_call(
        functools.partial(kernel, kinds, names, sum(1 << part for part in ready), fill, name != "last"),
        out_shape=[
            jax.ShapeDtypeStruct((chans, slots, 2, rows, rows), jnp.bfloat16),
            pltpu.VMEM((16, HALF, width), jnp.bfloat16),
        ],
        in_specs=specs,
        out_specs=[whole, vector],
        input_output_aliases=aliases,
        scratch_shapes=[
            pltpu.SMEM((2,), jnp.int32),
            pltpu.VMEM((2, 2, HALF, rows), jnp.bfloat16),
            pltpu.VMEM((2, 2, rows, HALF), jnp.bfloat16),
            pltpu.VMEM((2, 2, rows, rows), jnp.bfloat16),
            pltpu.SemaphoreType.DMA((16,)),
            pltpu.SemaphoreType.DMA((2,)),
        ],
        compiler_params=pltpu.CompilerParams(vmem_limit_bytes=STAGE_VMEM),
        cost_estimate=pl.CostEstimate(flops=weight, bytes_accessed=weight, transcendentals=0),
        name=name,
    )(*operands)


def cut_kernel(cuts, step, beams, *refs):
    outs, (held, in_sems, out_sems) = refs[: len(cuts)], refs[len(cuts) :]
    pos, many = lax.axis_index("ma"), lax.axis_size("ma")
    inward, outward = [], []
    for (shift, first, height), out in zip(cuts, outs):
        block = beams.at[lax.rem(pos + shift, many)]
        for row in range(0, height, step):
            part = len(inward)
            inward.append(pltpu.make_async_copy(block.at[pl.ds(first + row, step)], held.at[part], in_sems.at[part]))
            outward.append(pltpu.make_async_copy(held.at[part], out.at[pl.ds(row, step)], out_sems.at[part]))
    for copy in inward:
        copy.start()
    for there, back in zip(inward, outward):
        there.wait()
        back.start()
    for copy in outward:
        copy.wait()


def cut_kernel_near(cuts, step, beams, *refs):
    outs, sems = refs[: len(cuts)], refs[len(cuts)]
    pos, many = lax.axis_index("ma"), lax.axis_size("ma")
    copies = []
    for (shift, first, height), out in zip(cuts, outs):
        block = beams.at[lax.rem(pos + shift, many)]
        for row in range(0, height, step):
            source, sem = block.at[pl.ds(first + row, step)], sems.at[len(copies)]
            copies.append(pltpu.make_async_copy(source, out.at[pl.ds(row, step)], sem))
    for copy in copies:
        copy.start()
    for copy in copies:
        copy.wait()


def cut_near(beams, *cuts):
    step = 64
    parts = sum(height for _, _, height in cuts) // step
    return pl.pallas_call(
        functools.partial(cut_kernel_near, cuts, step),
        out_shape=[pltpu.VMEM((height, beams.shape[2]), beams.dtype) for _, _, height in cuts],
        in_specs=[pl.BlockSpec(memory_space=pl.ANY)],
        out_specs=[pl.BlockSpec(memory_space=pltpu.VMEM)] * len(cuts),
        scratch_shapes=[pltpu.SemaphoreType.DMA((parts,))],
        compiler_params=pltpu.CompilerParams(vmem_limit_bytes=VMEM),
        cost_estimate=pl.CostEstimate(flops=10**12, bytes_accessed=1, transcendentals=0),
        name="near",
    )(beams)


def cut_out(beams, *cuts):
    step = 32
    parts = sum(height for _, _, height in cuts) // step
    whole = pl.BlockSpec(memory_space=pl.ANY)
    return pl.pallas_call(
        functools.partial(cut_kernel, cuts, step),
        out_shape=[jax.ShapeDtypeStruct((height, beams.shape[2]), beams.dtype) for _, _, height in cuts],
        in_specs=[whole],
        out_specs=[whole] * len(cuts),
        scratch_shapes=[
            pltpu.VMEM((parts, step, beams.shape[2]), beams.dtype),
            pltpu.SemaphoreType.DMA((parts,)),
            pltpu.SemaphoreType.DMA((parts,)),
        ],
        compiler_params=pltpu.CompilerParams(vmem_limit_bytes=VMEM),
        cost_estimate=pl.CostEstimate(flops=10**12, bytes_accessed=1, transcendentals=0),
        name="cut",
    )(beams)


def along(array, by):
    count = lax.axis_size("ma")
    return lax.ppermute(array, "ma", [(i, (i + by) % count) for i in range(count)])


def beside(array, source, per_band):
    many, groups = lax.axis_size("ma"), lax.axis_size("af")
    pairs = []
    for pos in range(many):
        for group in range(groups):
            channel = (pos + source) % many
            target = group + 1 if channel >= many // 2 else group - 1
            if 0 <= target < groups and target // per_band == group // per_band:
                pairs.append((pos * groups + group, pos * groups + target))
    return lax.ppermute(array, ("ma", "af"), pairs)


def body(beams, spectrum, partners):
    many, _, _, rows, width = beams.shape
    per_band = BAND // many
    beams = beams.reshape(many, rows, width)

    down, up = [None, None], [None, None]
    down[0], up[0] = cut_near(beams, (3, 0, NEAR), (1, 0, NEAR))
    again, down[0], up[0] = ORDER((beams, down[0], up[0]))
    down[1], up[1] = cut_near(again, (3, NEAR, rows - NEAR), (1, NEAR, rows - NEAR))
    again, down[1], up[1] = ORDER((beams, down[1], up[1]))
    own, far0, far1 = cut_out(again, (0, 0, rows), (2, 0, FIRST_ROWS), (2, FIRST_ROWS, rows - FIRST_ROWS))
    plan = make_plan(partners, CAPS)

    near1 = [along(part, -1) for part in down]
    near3 = [along(part, 1) for part in up]
    side0 = beside(own, 0, per_band)
    side1 = [beside(near1[0], 1, per_band)]
    side3 = [beside(near3[0], 3, per_band)]
    far0, near1[1], side1[0], side3[0] = ORDER((far0, near1[1], side1[0], side3[0]))
    late0 = along(far0, 2)
    far1, near1[1], near3[1], side0 = ORDER((far1, near1[1], near3[1], side0))
    late1 = along(far1, 2)
    side1.append(beside(near1[1], 1, per_band))
    side3.append(beside(near3[1], 3, per_band))

    ready, fill = (), (0, 1, 2, 3, 6, 7, 8, 9)
    pieces = {(0, 0): beams, (4, 0): side0}
    pieces |= {(1, 0): near1[0], (1, NEAR): near1[1], (3, 0): near3[0], (3, NEAR): near3[1]}
    out, held = run_stage("early", (2,), plan[0], spectrum, pieces, ready, fill, None, None, WEIGHTS[0])

    late0, out = ORDER((late0, out))
    side_first = beside(late0, 2, per_band)
    ready, fill = ready + fill, (4, 10, 11, 14, 15)
    pieces = {(2, 0): late0, (5, 0): side1[0], (5, NEAR): side1[1], (7, 0): side3[0], (7, NEAR): side3[1]}
    out, held = run_stage("middle", (0, 1, 2), plan[1], spectrum, pieces, ready, fill, held, out, WEIGHTS[1])

    late1, out = ORDER((late1, out))
    side_second = beside(late1, 2, per_band)
    side_first, out = ORDER((side_first, out))
    ready, fill = ready + fill, (5, 12)
    pieces = {(2, 0): late0, (2, FIRST_ROWS): late1, (6, 0): side_first}
    out, held = run_stage("late", (0, 1, 2), plan[2], spectrum, pieces, ready, fill, held, out, WEIGHTS[2])

    side_second, out = ORDER((side_second, out))
    ready, fill = ready + fill, (13,)
    pieces = {(6, 0): side_first, (6, FIRST_ROWS): side_second}
    out, held = run_stage("last", (1,), plan[3], spectrum, pieces, ready, fill, held, out, WEIGHTS[3])
    return out[None]


def solution(mesh):
    in_specs = (P(None, "af", "ma", None, None), P("af", None, None), P("af", None))
    out_specs = P("ma", "af", None, None, None, None)
    return jax.shard_map(body, mesh=mesh, in_specs=in_specs, out_specs=out_specs, check_vma=False)
```

profile of v0, /device:TPU:113, one launch (start us, length us, event | category | flops | bytes accessed | tf_op | source)
XLA Modules:
  0.0 128.1 jit_solution(631321010766201652)
XLA Ops:
  0.0 2.2 %near.2 = (bf16[128,2048]{1,0:T(8,128)(2,1)}, bf16[128,2048]{1,0:T(8,128)(2,1)}) custom-call(bf16[4,512,2048]{2,1,0:T(8,128)(2,1)} %bitcast.2), custom_call_target="tpu_custom_call" | custom-call | flops 999999995904 | bytes 1 | tf_op jit(solution)/shard_map/near/pallas_call | solution.py:293
  2.2 0.2 collective-permute-start.1
  2.4 1.3 %collective-permute-start.3 = (bf16[128,2048]{1,0:T(8,128)(2,1)}, bf16[128,2048]{1,0:T(8,128)(2,1)}, u32[]{:S(2)}, u32[]{:S(2)}) collective-permute-start(bf16[128,2048]{1,0:T(8,128)(2,1)} %get-tuple-element.55), channel_id=1, source_target_pairs={{0,32},{32,64},{64,96},{96,0},{1,33},{33,65},{65,97},{97,1},{2,34}... | collective-permute-start | bytes 1572872 | tf_op jit(solution)/shard_map/ppermute | solution.py:327
  3.7 3.6 %near.3 = (bf16[384,2048]{1,0:T(8,128)(2,1)}, bf16[384,2048]{1,0:T(8,128)(2,1)}) custom-call(bf16[4,512,2048]{2,1,0:T(8,128)(2,1)} %bitcast.3), custom_call_target="tpu_custom_call" | custom-call | flops 999999995904 | bytes 1 | tf_op jit(solution)/shard_map/near/pallas_call | solution.py:293
  7.4 0.2 collective-permute-start
  7.6 2.1 %collective-permute-start.6 = (bf16[384,2048]{1,0:T(8,128)(2,1)}, bf16[384,2048]{1,0:T(8,128)(2,1)}, u32[]{:S(2)}, u32[]{:S(2)}) collective-permute-start(bf16[384,2048]{1,0:T(8,128)(2,1)} %get-tuple-element.60), channel_id=1, source_target_pairs={{0,32},{32,64},{64,96},{96,0},{1,33},{33,65},{65,97},{97,1},{2,34}... | collective-permute-start | bytes 4718600 | tf_op jit(solution)/shard_map/ppermute | solution.py:327
  9.7 4.5 %cut.1 = (bf16[512,2048]{1,0:T(8,128)(2,1)}, bf16[256,2048]{1,0:T(8,128)(2,1)}, bf16[256,2048]{1,0:T(8,128)(2,1)}) custom-call(bf16[4,512,2048]{2,1,0:T(8,128)(2,1)} %bitcast.4), custom_call_target="tpu_custom_call" | custom-call | flops 999999995904 | bytes 1 | tf_op jit(solution)/shard_map/cut/pallas_call | solution.py:309
  14.2 3.2 %collective-permute-start.7 = (bf16[512,2048]{1,0:T(8,128)(2,1)}, bf16[512,2048]{1,0:T(8,128)(2,1)}, u32[]{:S(2)}, u32[]{:S(2)}) collective-permute-start(bf16[512,2048]{1,0:T(8,128)(2,1)} %get-tuple-element.61), channel_id=1, source_target_pairs={{1,0},{2,1},{3,2},{4,3},{5,4},{6,5},{7,6},{8,7},{9,8},{10,9},{11,1... | collective-permute-start | bytes 6291464 | tf_op jit(solution)/shard_map/ppermute | solution.py:339
  17.4 0.0 collective-permute-done.1.refs_4_
  17.4 2.3 %collective-permute-start.2 = (bf16[128,2048]{1,0:T(8,128)(2,1)}, bf16[128,2048]{1,0:T(8,128)(2,1)}, u32[]{:S(2)}, u32[]{:S(2)}) collective-permute-start(bf16[128,2048]{1,0:T(8,128)(2,1)} %collective-permute-done.1.refs_4_), channel_id=1, source_target_pairs={{1,0},{2,1},{3,2},{4,3},{5,4},{6,5},{7,6},{8,7},{9,8},{10,9},{11,1... | collective-permute-start | bytes 1572872 | tf_op jit(solution)/shard_map/ppermute | solution.py:339
  19.7 0.0 collective-permute-done.3.refs_6_
  19.7 2.2 %collective-permute-start.4 = (bf16[128,2048]{1,0:T(8,128)(2,1)}, bf16[128,2048]{1,0:T(8,128)(2,1)}, u32[]{:S(2)}, u32[]{:S(2)}) collective-permute-start(bf16[128,2048]{1,0:T(8,128)(2,1)} %collective-permute-done.3.refs_6_), channel_id=1, source_target_pairs={{0,1},{1,2},{2,3},{3,4},{4,5},{5,6},{6,7},{7,8},{8,9},{9,10},{10,1... | collective-permute-start | bytes 1572872 | tf_op jit(solution)/shard_map/ppermute | solution.py:339
  21.9 0.0 copy-start
  21.9 3.7 %plan.1 = (s32[25,7]{1,0:T(8,128)}, s32[25,7]{1,0:T(8,128)}, s32[25,7]{1,0:T(8,128)}, s32[25,7]{1,0:T(8,128)}) custom-call(s32[4,3]{1,0:T(4,128)} %partners.1), custom_call_target="tpu_custom_call" | custom-call | flops 999999995904 | bytes 1 | tf_op jit(solution)/shard_map/plan/pallas_call | solution.py:88
  25.6 0.0 copy-done
  25.6 0.7 copy.13.refs_1_
  26.3 20.0 %collective-permute-done.2.refs_3_ = bf16[128,2048]{1,0:T(8,128)(2,1)} collective-permute-done((bf16[128,2048]{1,0:T(8,128)(2,1)}, bf16[128,2048]{1,0:T(8,128)(2,1)}, u32[]{:S(2)}, u32[]{:S(2)}) %collective-permute-start.2) | collective-permute-done | bytes 524320 | tf_op jit(solution)/shard_map/ppermute | solution.py:339
  46.3 0.0 collective-permute-done.4.refs_5_
  46.3 2.8 %collective-permute-done.refs_5_ = bf16[384,2048]{1,0:T(8,128)(2,1)} collective-permute-done((bf16[384,2048]{1,0:T(8,128)(2,1)}, bf16[384,2048]{1,0:T(8,128)(2,1)}, u32[]{:S(2)}, u32[]{:S(2)}) %collective-permute-start) | collective-permute-done | bytes 1572896 | tf_op jit(solution)/shard_map/ppermute | solution.py:327
  49.1 2.3 %collective-permute-start.5 = (bf16[256,2048]{1,0:T(8,128)(2,1)}, bf16[256,2048]{1,0:T(8,128)(2,1)}, u32[]{:S(2)}, u32[]{:S(2)}) collective-permute-start(bf16[256,2048]{1,0:T(8,128)(2,1)} %get-tuple-element.56), channel_id=1, source_target_pairs={{0,64},{32,96},{64,0},{96,32},{1,65},{33,97},{65,1},{97,33},{2,66}... | collective-permute-start | bytes 3145736 | tf_op jit(solution)/shard_map/ppermute | solution.py:327
  51.4 0.0 collective-permute-done.6.refs_7_
  51.4 0.0 collective-permute-done.7.refs_3_
  51.4 1.4 %collective-permute-start.9 = (bf16[256,2048]{1,0:T(8,128)(2,1)}, bf16[256,2048]{1,0:T(8,128)(2,1)}, u32[]{:S(2)}, u32[]{:S(2)}) collective-permute-start(bf16[256,2048]{1,0:T(8,128)(2,1)} %get-tuple-element.67), channel_id=1, source_target_pairs={{0,64},{32,96},{64,0},{96,32},{1,65},{33,97},{65,1},{97,33},{2,66}... | collective-permute-start | bytes 3145736 | tf_op jit(solution)/shard_map/ppermute | solution.py:327
  52.8 3.8 %collective-permute-start.10 = (bf16[384,2048]{1,0:T(8,128)(2,1)}, bf16[384,2048]{1,0:T(8,128)(2,1)}, u32[]{:S(2)}, u32[]{:S(2)}) collective-permute-start(bf16[384,2048]{1,0:T(8,128)(2,1)} %collective-permute-done.refs_5_), channel_id=1, source_target_pairs={{1,0},{2,1},{3,2},{4,3},{5,4},{6,5},{7,6},{8,7},{9,8},{10,9},{11,1... | collective-permute-start | bytes 4718600 | tf_op jit(solution)/shard_map/ppermute | solution.py:339
  56.6 2.2 %collective-permute-start.11 = (bf16[384,2048]{1,0:T(8,128)(2,1)}, bf16[384,2048]{1,0:T(8,128)(2,1)}, u32[]{:S(2)}, u32[]{:S(2)}) collective-permute-start(bf16[384,2048]{1,0:T(8,128)(2,1)} %collective-permute-done.6.refs_7_), channel_id=1, source_target_pairs={{0,1},{1,2},{2,3},{3,4},{4,5},{5,6},{6,7},{7,8},{8,9},{9,10},{10,1... | collective-permute-start | bytes 4718600 | tf_op jit(solution)/shard_map/ppermute | solution.py:339
  58.8 11.4 %early.1 = (bf16[4,3,2,512,512]{4,3,2,1,0:T(8,128)(2,1)}, bf16[16,256,2048]{2,1,0:T(8,128)(2,1)S(1)}) custom-call(s32[25,7]{1,0:T(8,128)} %get-tuple-element.57.refs_0_, f32[4,3,1024]{2,1,0:T(4,128)} %copy.13.refs_1_, bf16[4,512,2048]{2,1,0:T(8,128)(2,1)} %bitcast.5, bf16[512,2048]{1,0:T(8,128)(2,1)} %collective-permute-done.7.refs_3_, ...), custom_call_target="tpu_custom_call" | custom-call | flops 999999995904 | bytes 999999995904 | tf_op jit(solution)/shard_map/early/pallas_call | solution.py:233
  70.2 4.1 %collective-permute-done.5.refs_2_ = bf16[256,2048]{1,0:T(8,128)(2,1)} collective-permute-done((bf16[256,2048]{1,0:T(8,128)(2,1)}, bf16[256,2048]{1,0:T(8,128)(2,1)}, u32[]{:S(2)}, u32[]{:S(2)}) %collective-permute-start.5) | collective-permute-done | bytes 1048608 | tf_op jit(solution)/shard_map/ppermute | solution.py:327
  74.3 6.1 %collective-permute-start.8 = (bf16[256,2048]{1,0:T(8,128)(2,1)}, bf16[256,2048]{1,0:T(8,128)(2,1)}, u32[]{:S(2)}, u32[]{:S(2)}) collective-permute-start(bf16[256,2048]{1,0:T(8,128)(2,1)} %collective-permute-done.5.refs_2_), channel_id=1, source_target_pairs={{0,1},{1,2},{2,3},{3,4},{4,5},{5,6},{6,7},{7,8},{8,9},{9,10},{10,1... | collective-permute-start | bytes 3145736 | tf_op jit(solution)/shard_map/ppermute | solution.py:339
  80.5 0.0 collective-permute-done.10.refs_4_
  80.5 0.3 collective-permute-done.11.refs_6_
  80.7 5.8 %middle.1 = (bf16[4,3,2,512,512]{4,3,2,1,0:T(8,128)(2,1)}, bf16[16,256,2048]{2,1,0:T(8,128)(2,1)S(1)}) custom-call(s32[25,7]{1,0:T(8,128)} %get-tuple-element.68.refs_0_, f32[4,3,1024]{2,1,0:T(4,128)} %copy.13.refs_1_, bf16[256,2048]{1,0:T(8,128)(2,1)} %collective-permute-done.5.refs_2_, ...), custom_call_target="tpu_custom_call", output_to_operand_aliasing={{0}: (7, {}), {1}: (8, {})} | custom-call | flops 999999995904 | bytes 999999995904 | tf_op jit(solution)/shard_map/middle/pallas_call | solution.py:233
  86.5 10.3 %collective-permute-done.9.refs_3_ = bf16[256,2048]{1,0:T(8,128)(2,1)} collective-permute-done((bf16[256,2048]{1,0:T(8,128)(2,1)}, bf16[256,2048]{1,0:T(8,128)(2,1)}, u32[]{:S(2)}, u32[]{:S(2)}) %collective-permute-start.9) | collective-permute-done | bytes 1048608 | tf_op jit(solution)/shard_map/ppermute | solution.py:327
  96.8 4.0 %collective-permute-start.12 = (bf16[256,2048]{1,0:T(8,128)(2,1)}, bf16[256,2048]{1,0:T(8,128)(2,1)}, u32[]{:S(2)}, u32[]{:S(2)}) collective-permute-start(bf16[256,2048]{1,0:T(8,128)(2,1)} %collective-permute-done.9.refs_3_), channel_id=1, source_target_pairs={{0,1},{1,2},{2,3},{3,4},{4,5},{5,6},{6,7},{7,8},{8,9},{9,10},{10,1... | collective-permute-start | bytes 3145736 | tf_op jit(solution)/shard_map/ppermute | solution.py:339
  100.9 0.0 collective-permute-done.8.refs_4_.refs_2_
  100.9 17.3 %late.1 = (bf16[4,3,2,512,512]{4,3,2,1,0:T(8,128)(2,1)}, bf16[16,256,2048]{2,1,0:T(8,128)(2,1)S(1)}) custom-call(s32[25,7]{1,0:T(8,128)} %get-tuple-element.77.refs_0_, f32[4,3,1024]{2,1,0:T(4,128)} %copy.13.refs_1_, bf16[256,2048]{1,0:T(8,128)(2,1)} %collective-permute-done.5.refs_2_, ...), custom_call_target="tpu_custom_call", output_to_operand_aliasing={{0}: (5, {}), {1}: (6, {})} | custom-call | tf_op jit(solution)/shard_map/late/pallas_call | solution.py:233
  118.2 0.0 collective-permute-done.12.refs_3_
  118.2 9.7 %last.1 = (bf16[4,3,2,512,512]{4,3,2,1,0:T(8,128)(2,1)}, bf16[16,256,2048]{2,1,0:T(8,128)(2,1)S(1)}) custom-call(s32[25,7]{1,0:T(8,128)} %get-tuple-element.45.refs_0_, f32[4,3,1024]{2,1,0:T(4,128)} %copy.13.refs_1_, bf16[256,2048]{1,0:T(8,128)(2,1)} %collective-permute-done.8.refs_4_.refs_2_, ...), custom_call_target="tpu_custom_call", output_to_operand_aliasing={{0}: (4, {}), {1}: (5, {})} | custom-call | tf_op jit(solution)/shard_map/last/pallas_call | solution.py:233
Async XLA Ops:
  2.2 15.2 %collective-permute-start.1 = (bf16[128,2048]{1,0:T(8,128)(2,1)}, bf16[128,2048]{1,0:T(8,128)(2,1)}, u32[]{:S(2)}, u32[]{:S(2)}) collective-permute-start(bf16[128,2048]{1,0:T(8,128)(2,1)} %get-tuple-element.54), channel_id=1, source_target_pairs={{0,96},{32,0},{64,32},{96,64},{1,97},{33,1},{65,33},{97,65},{2,98}... | collective-permute-start | bytes 1572872 | tf_op jit(solution)/shard_map/ppermute | solution.py:327
  2.4 17.3 %collective-permute-start.3 = (bf16[128,2048]{1,0:T(8,128)(2,1)}, bf16[128,2048]{1,0:T(8,128)(2,1)}, u32[]{:S(2)}, u32[]{:S(2)}) collective-permute-start(bf16[128,2048]{1,0:T(8,128)(2,1)} %get-tuple-element.55), channel_id=1, source_target_pairs={{0,32},{32,64},{64,96},{96,0},{1,33},{33,65},{65,97},{97,1},{2,34}... | collective-permute-start | bytes 1572872 | tf_op jit(solution)/shard_map/ppermute | solution.py:327
  7.4 41.7 %collective-permute-start = (bf16[384,2048]{1,0:T(8,128)(2,1)}, bf16[384,2048]{1,0:T(8,128)(2,1)}, u32[]{:S(2)}, u32[]{:S(2)}) collective-permute-start(bf16[384,2048]{1,0:T(8,128)(2,1)} %get-tuple-element.53), channel_id=1, source_target_pairs={{0,96},{32,0},{64,32},{96,64},{1,97},{33,1},{65,33},{97,65},{2,98}... | collective-permute-start | bytes 4718600 | tf_op jit(solution)/shard_map/ppermute | solution.py:327
  7.6 43.8 %collective-permute-start.6 = (bf16[384,2048]{1,0:T(8,128)(2,1)}, bf16[384,2048]{1,0:T(8,128)(2,1)}, u32[]{:S(2)}, u32[]{:S(2)}) collective-permute-start(bf16[384,2048]{1,0:T(8,128)(2,1)} %get-tuple-element.60), channel_id=1, source_target_pairs={{0,32},{32,64},{64,96},{96,0},{1,33},{33,65},{65,97},{97,1},{2,34}... | collective-permute-start | bytes 4718600 | tf_op jit(solution)/shard_map/ppermute | solution.py:327
  14.2 37.1 %collective-permute-start.7 = (bf16[512,2048]{1,0:T(8,128)(2,1)}, bf16[512,2048]{1,0:T(8,128)(2,1)}, u32[]{:S(2)}, u32[]{:S(2)}) collective-permute-start(bf16[512,2048]{1,0:T(8,128)(2,1)} %get-tuple-element.61), channel_id=1, source_target_pairs={{1,0},{2,1},{3,2},{4,3},{5,4},{6,5},{7,6},{8,7},{9,8},{10,9},{11,1... | collective-permute-start | bytes 6291464 | tf_op jit(solution)/shard_map/ppermute | solution.py:339
  17.4 28.9 %collective-permute-start.2 = (bf16[128,2048]{1,0:T(8,128)(2,1)}, bf16[128,2048]{1,0:T(8,128)(2,1)}, u32[]{:S(2)}, u32[]{:S(2)}) collective-permute-start(bf16[128,2048]{1,0:T(8,128)(2,1)} %collective-permute-done.1.refs_4_), channel_id=1, source_target_pairs={{1,0},{2,1},{3,2},{4,3},{5,4},{6,5},{7,6},{8,7},{9,8},{10,9},{11,1... | collective-permute-start | bytes 1572872 | tf_op jit(solution)/shard_map/ppermute | solution.py:339
  19.7 26.6 %collective-permute-start.4 = (bf16[128,2048]{1,0:T(8,128)(2,1)}, bf16[128,2048]{1,0:T(8,128)(2,1)}, u32[]{:S(2)}, u32[]{:S(2)}) collective-permute-start(bf16[128,2048]{1,0:T(8,128)(2,1)} %collective-permute-done.3.refs_6_), channel_id=1, source_target_pairs={{0,1},{1,2},{2,3},{3,4},{4,5},{5,6},{6,7},{7,8},{8,9},{9,10},{10,1... | collective-permute-start | bytes 1572872 | tf_op jit(solution)/shard_map/ppermute | solution.py:339
  21.9 3.7 %copy-start = (f32[4,3,1024]{2,0,1:T(4,128)S(1)}, f32[4,3,1024]{2,0,1:T(4,128)}, u32[]{:S(2)}) copy-start(f32[4,3,1024]{2,0,1:T(4,128)} %param.4) | copy-start | bytes 147460
  49.1 25.2 %collective-permute-start.5 = (bf16[256,2048]{1,0:T(8,128)(2,1)}, bf16[256,2048]{1,0:T(8,128)(2,1)}, u32[]{:S(2)}, u32[]{:S(2)}) collective-permute-start(bf16[256,2048]{1,0:T(8,128)(2,1)} %get-tuple-element.56), channel_id=1, source_target_pairs={{0,64},{32,96},{64,0},{96,32},{1,65},{33,97},{65,1},{97,33},{2,66}... | collective-permute-start | bytes 3145736 | tf_op jit(solution)/shard_map/ppermute | solution.py:327
  51.4 45.4 %collective-permute-start.9 = (bf16[256,2048]{1,0:T(8,128)(2,1)}, bf16[256,2048]{1,0:T(8,128)(2,1)}, u32[]{:S(2)}, u32[]{:S(2)}) collective-permute-start(bf16[256,2048]{1,0:T(8,128)(2,1)} %get-tuple-element.67), channel_id=1, source_target_pairs={{0,64},{32,96},{64,0},{96,32},{1,65},{33,97},{65,1},{97,33},{2,66}... | collective-permute-start | bytes 3145736 | tf_op jit(solution)/shard_map/ppermute | solution.py:327
  52.8 27.7 %collective-permute-start.10 = (bf16[384,2048]{1,0:T(8,128)(2,1)}, bf16[384,2048]{1,0:T(8,128)(2,1)}, u32[]{:S(2)}, u32[]{:S(2)}) collective-permute-start(bf16[384,2048]{1,0:T(8,128)(2,1)} %collective-permute-done.refs_5_), channel_id=1, source_target_pairs={{1,0},{2,1},{3,2},{4,3},{5,4},{6,5},{7,6},{8,7},{9,8},{10,9},{11,1... | collective-permute-start | bytes 4718600 | tf_op jit(solution)/shard_map/ppermute | solution.py:339
  56.6 24.2 %collective-permute-start.11 = (bf16[384,2048]{1,0:T(8,128)(2,1)}, bf16[384,2048]{1,0:T(8,128)(2,1)}, u32[]{:S(2)}, u32[]{:S(2)}) collective-permute-start(bf16[384,2048]{1,0:T(8,128)(2,1)} %collective-permute-done.6.refs_7_), channel_id=1, source_target_pairs={{0,1},{1,2},{2,3},{3,4},{4,5},{5,6},{6,7},{7,8},{8,9},{9,10},{10,1... | collective-permute-start | bytes 4718600 | tf_op jit(solution)/shard_map/ppermute | solution.py:339
  74.3 26.5 %collective-permute-start.8 = (bf16[256,2048]{1,0:T(8,128)(2,1)}, bf16[256,2048]{1,0:T(8,128)(2,1)}, u32[]{:S(2)}, u32[]{:S(2)}) collective-permute-start(bf16[256,2048]{1,0:T(8,128)(2,1)} %collective-permute-done.5.refs_2_), channel_id=1, source_target_pairs={{0,1},{1,2},{2,3},{3,4},{4,5},{5,6},{6,7},{7,8},{8,9},{9,10},{10,1... | collective-permute-start | bytes 3145736 | tf_op jit(solution)/shard_map/ppermute | solution.py:339
  96.8 21.4 %collective-permute-start.12 = (bf16[256,2048]{1,0:T(8,128)(2,1)}, bf16[256,2048]{1,0:T(8,128)(2,1)}, u32[]{:S(2)}, u32[]{:S(2)}) collective-permute-start(bf16[256,2048]{1,0:T(8,128)(2,1)} %collective-permute-done.9.refs_3_), channel_id=1, source_target_pairs={{0,1},{1,2},{2,3},{3,4},{4,5},{5,6},{6,7},{7,8},{8,9},{9,10},{10,1... | collective-permute-start | bytes 3145736 | tf_op jit(solution)/shard_map/ppermute | solution.py:339
where the time goes:
time: 126 us; the launch traced here: 128 us
  Pallas kernels  58.2 us (46%)
  waiting for transfers between devices  37.5 us (30%)
  starting transfers between devices  31.3 us (25%)
    pallas_call x4, Pallas kernels, run_stage(): pl.pallas_call(functools.partial(kernel, kinds, names, sum((1 << part for...  44.2 us
    ppermute x7, starting transfers between devices, beside(): return lax.ppermute(array, ('ma', 'af'), pairs)  23.8 us
    ppermute x7, waiting for transfers between devices, beside(): return lax.ppermute(array, ('ma', 'af'), pairs)  20.3 us
    ppermute x6, waiting for transfers between devices, along(): lax.ppermute(array, 'ma', [(i, (i + by) % count) for i in range(count)])  17.2 us
    ppermute x6, starting transfers between devices, along(): lax.ppermute(array, 'ma', [(i, (i + by) % count) for i in range(count)])  7.58 us
    pallas_call x2, Pallas kernels, cut_near(): pl.pallas_call(functools.partial(cut_kernel_near, cuts, step), out_shape=...  5.81 us
    pallas_call x1, Pallas kernels, cut_out(): pl.pallas_call(functools.partial(cut_kernel, cuts, step), out_shape=[jax....  4.51 us
    pallas_call x1, Pallas kernels, make_plan(): pl.pallas_call(functools.partial(plan_kernel, stages, caps), out_shape=[j...  3.65 us
  transfers between devices with their start and end apart: 13, of which 5 were waited for; matrix products, arithmetic and copies ran while one was open for 1% of the time, Pallas kernels for 36%

commit v1 on v0

--- a/solution.py
+++ b/solution.py
@@ -345,7 +345,10 @@
     beams = beams.reshape(many, rows, width)
 
     down, up = [None, None], [None, None]
-    down[0], up[0] = cut_near(beams, (3, 0, NEAR), (1, 0, NEAR))
+    pos = lax.axis_index("ma")
+    down[0], up[0] = (
+        lax.dynamic_slice(beams, (lax.rem(pos + shift, many), 0, 0), (1, NEAR, width))[0] for shift in (3, 1)
+    )
     again, down[0], up[0] = ORDER((beams, down[0], up[0]))
     down[1], up[1] = cut_near(again, (3, NEAR, rows - NEAR), (1, NEAR, rows - NEAR))
     again, down[1], up[1] = ORDER((beams, down[1], up[1]))

time: 126 us -> 125 us (level)
  the two profiles are of different devices: /device:TPU:113 before, /device:TPU:6 now
where the time goes in v1:
time: 125 us; the launch traced here: 123 us
  Pallas kernels  54.8 us (44%)
  waiting for transfers between devices  34.5 us (28%)
  starting transfers between devices  30.9 us (25%)
  local copies, waits for them, and re-layouts  2.95 us (2%)
    pallas_call x4, Pallas kernels, run_stage(): pl.pallas_call(functools.partial(kernel, kinds, names, sum((1 << part for...  43 us
    ppermute x7, waiting for transfers between devices, beside(): return lax.ppermute(array, ('ma', 'af'), pairs)  31.5 us
    ppermute x7, starting transfers between devices, beside(): return lax.ppermute(array, ('ma', 'af'), pairs)  21.3 us
    ppermute x6, starting transfers between devices, along(): lax.ppermute(array, 'ma', [(i, (i + by) % count) for i in range(count)])  9.64 us
    pallas_call x1, Pallas kernels, cut_out(): pl.pallas_call(functools.partial(cut_kernel, cuts, step), out_shape=[jax....  4.51 us
    pallas_call x1, Pallas kernels, make_plan(): pl.pallas_call(functools.partial(plan_kernel, stages, caps), out_shape=[j...  3.65 us
    pallas_call x1, Pallas kernels, cut_near(): pl.pallas_call(functools.partial(cut_kernel_near, cuts, step), out_shape=...  3.62 us
    ppermute x6, waiting for transfers between devices, along(): lax.ppermute(array, 'ma', [(i, (i + by) % count) for i in range(count)])  3.01 us
  transfers between devices with their start and end apart: 13, of which 6 were waited for; matrix products, arithmetic and copies ran while one was open for 1% of the time, Pallas kernels for 41%

profile of v1, /device:TPU:6, one launch (start us, length us, event | category | flops | bytes accessed | tf_op | source)
XLA Modules:
  0.0 123.5 jit_solution(3617788188114071320)
XLA Ops:
  0.0 2.3 %dynamic-slice_bitcast_fusion = (bf16[128,2048]{1,0:T(8,128)(2,1)}, bf16[128,2048]{1,0:T(8,128)(2,1)}) fusion(bf16[4,1,1,512,2048]{4,3,2,1,0:T(8,128)(2,1)} %param.3, s32[]{:T(128)S(6)} %select_n.7, s32[]{:T(128)S(6)} %select_n.6), kind=kLoop, calls=%fused_computation | loop fusion | bytes 2097160 | tf_op jit(solution)/shard_map/squeeze | solution.py:350
  2.3 3.0 %collective-permute-start.1 = (bf16[128,2048]{1,0:T(8,128)(2,1)}, bf16[128,2048]{1,0:T(8,128)(2,1)}, u32[]{:S(2)}, u32[]{:S(2)}) collective-permute-start(bf16[128,2048]{1,0:T(8,128)(2,1)} %get-tuple-element.50), channel_id=1, source_target_pairs={{0,96},{32,0},{64,32},{96,64},{1,97},{33,1},{65,33},{97,65},{2,98}... | collective-permute-start | bytes 1572872 | tf_op jit(solution)/shard_map/ppermute | solution.py:327
  5.3 0.0 collective-permute-start.3
  5.3 3.6 %near.1 = (bf16[384,2048]{1,0:T(8,128)(2,1)}, bf16[384,2048]{1,0:T(8,128)(2,1)}) custom-call(bf16[4,512,2048]{2,1,0:T(8,128)(2,1)} %bitcast.6), custom_call_target="tpu_custom_call" | custom-call | flops 999999995904 | bytes 1 | tf_op jit(solution)/shard_map/near/pallas_call | solution.py:293
  8.9 3.3 %collective-permute-start = (bf16[384,2048]{1,0:T(8,128)(2,1)}, bf16[384,2048]{1,0:T(8,128)(2,1)}, u32[]{:S(2)}, u32[]{:S(2)}) collective-permute-start(bf16[384,2048]{1,0:T(8,128)(2,1)} %get-tuple-element.49), channel_id=1, source_target_pairs={{0,96},{32,0},{64,32},{96,64},{1,97},{33,1},{65,33},{97,65},{2,98}... | collective-permute-start | bytes 4718600 | tf_op jit(solution)/shard_map/ppermute | solution.py:327
  12.2 0.0 collective-permute-start.6
  12.2 4.5 %cut.1 = (bf16[512,2048]{1,0:T(8,128)(2,1)}, bf16[256,2048]{1,0:T(8,128)(2,1)}, bf16[256,2048]{1,0:T(8,128)(2,1)}) custom-call(bf16[4,512,2048]{2,1,0:T(8,128)(2,1)} %bitcast.7), custom_call_target="tpu_custom_call" | custom-call | flops 999999995904 | bytes 1 | tf_op jit(solution)/shard_map/cut/pallas_call | solution.py:309
  16.7 4.8 %collective-permute-start.7 = (bf16[512,2048]{1,0:T(8,128)(2,1)}, bf16[512,2048]{1,0:T(8,128)(2,1)}, u32[]{:S(2)}, u32[]{:S(2)}) collective-permute-start(bf16[512,2048]{1,0:T(8,128)(2,1)} %get-tuple-element.57), channel_id=1, source_target_pairs={{1,0},{2,1},{3,2},{4,3},{5,4},{6,5},{7,6},{8,7},{9,8},{10,9},{11,1... | collective-permute-start | bytes 6291464 | tf_op jit(solution)/shard_map/ppermute | solution.py:339
  21.6 0.0 collective-permute-done.1.refs_4_
  21.6 3.4 %collective-permute-start.2 = (bf16[128,2048]{1,0:T(8,128)(2,1)}, bf16[128,2048]{1,0:T(8,128)(2,1)}, u32[]{:S(2)}, u32[]{:S(2)}) collective-permute-start(bf16[128,2048]{1,0:T(8,128)(2,1)} %collective-permute-done.1.refs_4_), channel_id=1, source_target_pairs={{1,0},{2,1},{3,2},{4,3},{5,4},{6,5},{7,6},{8,7},{9,8},{10,9},{11,1... | collective-permute-start | bytes 1572872 | tf_op jit(solution)/shard_map/ppermute | solution.py:339
  25.0 0.0 collective-permute-done.3.refs_6_
  25.0 1.9 %collective-permute-start.4 = (bf16[128,2048]{1,0:T(8,128)(2,1)}, bf16[128,2048]{1,0:T(8,128)(2,1)}, u32[]{:S(2)}, u32[]{:S(2)}) collective-permute-start(bf16[128,2048]{1,0:T(8,128)(2,1)} %collective-permute-done.3.refs_6_), channel_id=1, source_target_pairs={{0,1},{1,2},{2,3},{3,4},{4,5},{5,6},{6,7},{7,8},{8,9},{9,10},{10,1... | collective-permute-start | bytes 1572872 | tf_op jit(solution)/shard_map/ppermute | solution.py:339
  26.9 0.0 copy-start
  27.0 3.7 %plan.1 = (s32[25,7]{1,0:T(8,128)}, s32[25,7]{1,0:T(8,128)}, s32[25,7]{1,0:T(8,128)}, s32[25,7]{1,0:T(8,128)}) custom-call(s32[4,3]{1,0:T(4,128)} %partners.1), custom_call_target="tpu_custom_call" | custom-call | flops 999999995904 | bytes 1 | tf_op jit(solution)/shard_map/plan/pallas_call | solution.py:88
  30.6 0.0 copy-done
  30.6 0.7 copy.13.refs_1_
  31.3 19.7 %collective-permute-done.2.refs_3_ = bf16[128,2048]{1,0:T(8,128)(2,1)} collective-permute-done((bf16[128,2048]{1,0:T(8,128)(2,1)}, bf16[128,2048]{1,0:T(8,128)(2,1)}, u32[]{:S(2)}, u32[]{:S(2)}) %collective-permute-start.2) | collective-permute-done | bytes 524320 | tf_op jit(solution)/shard_map/ppermute | solution.py:339
  51.0 0.0 collective-permute-done.4.refs_5_
  51.0 0.0 collective-permute-done.refs_5_
  51.0 2.7 %collective-permute-start.5 = (bf16[256,2048]{1,0:T(8,128)(2,1)}, bf16[256,2048]{1,0:T(8,128)(2,1)}, u32[]{:S(2)}, u32[]{:S(2)}) collective-permute-start(bf16[256,2048]{1,0:T(8,128)(2,1)} %get-tuple-element.52), channel_id=1, source_target_pairs={{0,64},{32,96},{64,0},{96,32},{1,65},{33,97},{65,1},{97,33},{2,66}... | collective-permute-start | bytes 3145736 | tf_op jit(solution)/shard_map/ppermute | solution.py:327
  53.7 0.2 collective-permute-done.6.refs_7_
  53.9 0.0 collective-permute-done.7.refs_3_
  53.9 0.7 collective-permute-start.9
  54.6 5.4 %collective-permute-start.10 = (bf16[384,2048]{1,0:T(8,128)(2,1)}, bf16[384,2048]{1,0:T(8,128)(2,1)}, u32[]{:S(2)}, u32[]{:S(2)}) collective-permute-start(bf16[384,2048]{1,0:T(8,128)(2,1)} %collective-permute-done.refs_5_), channel_id=1, source_target_pairs={{1,0},{2,1},{3,2},{4,3},{5,4},{6,5},{7,6},{8,7},{9,8},{10,9},{11,1... | collective-permute-start | bytes 4718600 | tf_op jit(solution)/shard_map/ppermute | solution.py:339
  59.9 1.9 %collective-permute-start.11 = (bf16[384,2048]{1,0:T(8,128)(2,1)}, bf16[384,2048]{1,0:T(8,128)(2,1)}, u32[]{:S(2)}, u32[]{:S(2)}) collective-permute-start(bf16[384,2048]{1,0:T(8,128)(2,1)} %collective-permute-done.6.refs_7_), channel_id=1, source_target_pairs={{0,1},{1,2},{2,3},{3,4},{4,5},{5,6},{6,7},{7,8},{8,9},{9,10},{10,1... | collective-permute-start | bytes 4718600 | tf_op jit(solution)/shard_map/ppermute | solution.py:339
  61.9 15.6 %early.1 = (bf16[4,3,2,512,512]{4,3,2,1,0:T(8,128)(2,1)}, bf16[16,256,2048]{2,1,0:T(8,128)(2,1)S(1)}) custom-call(s32[25,7]{1,0:T(8,128)} %get-tuple-element.53.refs_0_, f32[4,3,1024]{2,1,0:T(4,128)} %copy.13.refs_1_, bf16[4,512,2048]{2,1,0:T(8,128)(2,1)} %bitcast.8, bf16[512,2048]{1,0:T(8,128)(2,1)} %collective-permute-done.7.refs_3_, ...), custom_call_target="tpu_custom_call" | custom-call | flops 999999995904 | bytes 999999995904 | tf_op jit(solution)/shard_map/early/pallas_call | solution.py:233
  77.5 1.5 %collective-permute-done.5.refs_2_ = bf16[256,2048]{1,0:T(8,128)(2,1)} collective-permute-done((bf16[256,2048]{1,0:T(8,128)(2,1)}, bf16[256,2048]{1,0:T(8,128)(2,1)}, u32[]{:S(2)}, u32[]{:S(2)}) %collective-permute-start.5) | collective-permute-done | bytes 1048608 | tf_op jit(solution)/shard_map/ppermute | solution.py:327
  78.9 1.9 %collective-permute-start.8 = (bf16[256,2048]{1,0:T(8,128)(2,1)}, bf16[256,2048]{1,0:T(8,128)(2,1)}, u32[]{:S(2)}, u32[]{:S(2)}) collective-permute-start(bf16[256,2048]{1,0:T(8,128)(2,1)} %collective-permute-done.5.refs_2_), channel_id=1, source_target_pairs={{0,1},{1,2},{2,3},{3,4},{4,5},{5,6},{6,7},{7,8},{8,9},{9,10},{10,1... | collective-permute-start | bytes 3145736 | tf_op jit(solution)/shard_map/ppermute | solution.py:339
  80.9 0.0 collective-permute-done.10.refs_4_
  80.9 3.2 %collective-permute-done.11.refs_6_ = bf16[384,2048]{1,0:T(8,128)(2,1)} collective-permute-done((bf16[384,2048]{1,0:T(8,128)(2,1)}, bf16[384,2048]{1,0:T(8,128)(2,1)}, u32[]{:S(2)}, u32[]{:S(2)}) %collective-permute-start.11) | collective-permute-done | bytes 1572896 | tf_op jit(solution)/shard_map/ppermute | solution.py:339
  84.1 14.6 %middle.1 = (bf16[4,3,2,512,512]{4,3,2,1,0:T(8,128)(2,1)}, bf16[16,256,2048]{2,1,0:T(8,128)(2,1)S(1)}) custom-call(s32[25,7]{1,0:T(8,128)} %get-tuple-element.64.refs_0_, f32[4,3,1024]{2,1,0:T(4,128)} %copy.13.refs_1_, bf16[256,2048]{1,0:T(8,128)(2,1)} %collective-permute-done.5.refs_2_, ...), custom_call_target="tpu_custom_call", output_to_operand_aliasing={{0}: (7, {}), {1}: (8, {})} | custom-call | flops 999999995904 | bytes 999999995904 | tf_op jit(solution)/shard_map/middle/pallas_call | solution.py:233
  98.7 1.3 %collective-permute-done.9.refs_3_ = bf16[256,2048]{1,0:T(8,128)(2,1)} collective-permute-done((bf16[256,2048]{1,0:T(8,128)(2,1)}, bf16[256,2048]{1,0:T(8,128)(2,1)}, u32[]{:S(2)}, u32[]{:S(2)}) %collective-permute-start.9) | collective-permute-done | bytes 1048608 | tf_op jit(solution)/shard_map/ppermute | solution.py:327
  100.0 1.9 %collective-permute-start.12 = (bf16[256,2048]{1,0:T(8,128)(2,1)}, bf16[256,2048]{1,0:T(8,128)(2,1)}, u32[]{:S(2)}, u32[]{:S(2)}) collective-permute-start(bf16[256,2048]{1,0:T(8,128)(2,1)} %collective-permute-done.9.refs_3_), channel_id=1, source_target_pairs={{0,1},{1,2},{2,3},{3,4},{4,5},{5,6},{6,7},{7,8},{8,9},{9,10},{10,1... | collective-permute-start | bytes 3145736 | tf_op jit(solution)/shard_map/ppermute | solution.py:339
  101.9 0.0 collective-permute-done.8.refs_4_.refs_2_
  101.9 8.4 %late.1 = (bf16[4,3,2,512,512]{4,3,2,1,0:T(8,128)(2,1)}, bf16[16,256,2048]{2,1,0:T(8,128)(2,1)S(1)}) custom-call(s32[25,7]{1,0:T(8,128)} %get-tuple-element.73.refs_0_, f32[4,3,1024]{2,1,0:T(4,128)} %copy.13.refs_1_, bf16[256,2048]{1,0:T(8,128)(2,1)} %collective-permute-done.5.refs_2_, ...), custom_call_target="tpu_custom_call", output_to_operand_aliasing={{0}: (5, {}), {1}: (6, {})} | custom-call | tf_op jit(solution)/shard_map/late/pallas_call | solution.py:233
  110.4 8.5 %collective-permute-done.12.refs_3_ = bf16[256,2048]{1,0:T(8,128)(2,1)} collective-permute-done((bf16[256,2048]{1,0:T(8,128)(2,1)}, bf16[256,2048]{1,0:T(8,128)(2,1)}, u32[]{:S(2)}, u32[]{:S(2)}) %collective-permute-start.12) | collective-permute-done | bytes 1048608 | tf_op jit(solution)/shard_map/ppermute | solution.py:339
  118.9 4.4 %last.1 = (bf16[4,3,2,512,512]{4,3,2,1,0:T(8,128)(2,1)}, bf16[16,256,2048]{2,1,0:T(8,128)(2,1)S(1)}) custom-call(s32[25,7]{1,0:T(8,128)} %get-tuple-element.43.refs_0_, f32[4,3,1024]{2,1,0:T(4,128)} %copy.13.refs_1_, bf16[256,2048]{1,0:T(8,128)(2,1)} %collective-permute-done.8.refs_4_.refs_2_, ...), custom_call_target="tpu_custom_call", output_to_operand_aliasing={{0}: (4, {}), {1}: (5, {})} | custom-call | tf_op jit(solution)/shard_map/last/pallas_call | solution.py:233
Async XLA Ops:
  2.3 19.3 %collective-permute-start.1 = (bf16[128,2048]{1,0:T(8,128)(2,1)}, bf16[128,2048]{1,0:T(8,128)(2,1)}, u32[]{:S(2)}, u32[]{:S(2)}) collective-permute-start(bf16[128,2048]{1,0:T(8,128)(2,1)} %get-tuple-element.50), channel_id=1, source_target_pairs={{0,96},{32,0},{64,32},{96,64},{1,97},{33,1},{65,33},{97,65},{2,98}... | collective-permute-start | bytes 1572872 | tf_op jit(solution)/shard_map/ppermute | solution.py:327
  5.3 19.7 %collective-permute-start.3 = (bf16[128,2048]{1,0:T(8,128)(2,1)}, bf16[128,2048]{1,0:T(8,128)(2,1)}, u32[]{:S(2)}, u32[]{:S(2)}) collective-permute-start(bf16[128,2048]{1,0:T(8,128)(2,1)} %get-tuple-element.51), channel_id=1, source_target_pairs={{0,32},{32,64},{64,96},{96,0},{1,33},{33,65},{65,97},{97,1},{2,34}... | collective-permute-start | bytes 1572872 | tf_op jit(solution)/shard_map/ppermute | solution.py:327
  8.9 42.1 %collective-permute-start = (bf16[384,2048]{1,0:T(8,128)(2,1)}, bf16[384,2048]{1,0:T(8,128)(2,1)}, u32[]{:S(2)}, u32[]{:S(2)}) collective-permute-start(bf16[384,2048]{1,0:T(8,128)(2,1)} %get-tuple-element.49), channel_id=1, source_target_pairs={{0,96},{32,0},{64,32},{96,64},{1,97},{33,1},{65,33},{97,65},{2,98}... | collective-permute-start | bytes 4718600 | tf_op jit(solution)/shard_map/ppermute | solution.py:327
  12.2 41.7 %collective-permute-start.6 = (bf16[384,2048]{1,0:T(8,128)(2,1)}, bf16[384,2048]{1,0:T(8,128)(2,1)}, u32[]{:S(2)}, u32[]{:S(2)}) collective-permute-start(bf16[384,2048]{1,0:T(8,128)(2,1)} %get-tuple-element.56), channel_id=1, source_target_pairs={{0,32},{32,64},{64,96},{96,0},{1,33},{33,65},{65,97},{97,1},{2,34}... | collective-permute-start | bytes 4718600 | tf_op jit(solution)/shard_map/ppermute | solution.py:327
  16.7 37.2 %collective-permute-start.7 = (bf16[512,2048]{1,0:T(8,128)(2,1)}, bf16[512,2048]{1,0:T(8,128)(2,1)}, u32[]{:S(2)}, u32[]{:S(2)}) collective-permute-start(bf16[512,2048]{1,0:T(8,128)(2,1)} %get-tuple-element.57), channel_id=1, source_target_pairs={{1,0},{2,1},{3,2},{4,3},{5,4},{6,5},{7,6},{8,7},{9,8},{10,9},{11,1... | collective-permute-start | bytes 6291464 | tf_op jit(solution)/shard_map/ppermute | solution.py:339
  21.6 29.5 %collective-permute-start.2 = (bf16[128,2048]{1,0:T(8,128)(2,1)}, bf16[128,2048]{1,0:T(8,128)(2,1)}, u32[]{:S(2)}, u32[]{:S(2)}) collective-permute-start(bf16[128,2048]{1,0:T(8,128)(2,1)} %collective-permute-done.1.refs_4_), channel_id=1, source_target_pairs={{1,0},{2,1},{3,2},{4,3},{5,4},{6,5},{7,6},{8,7},{9,8},{10,9},{11,1... | collective-permute-start | bytes 1572872 | tf_op jit(solution)/shard_map/ppermute | solution.py:339
  25.0 26.0 %collective-permute-start.4 = (bf16[128,2048]{1,0:T(8,128)(2,1)}, bf16[128,2048]{1,0:T(8,128)(2,1)}, u32[]{:S(2)}, u32[]{:S(2)}) collective-permute-start(bf16[128,2048]{1,0:T(8,128)(2,1)} %collective-permute-done.3.refs_6_), channel_id=1, source_target_pairs={{0,1},{1,2},{2,3},{3,4},{4,5},{5,6},{6,7},{7,8},{8,9},{9,10},{10,1... | collective-permute-start | bytes 1572872 | tf_op jit(solution)/shard_map/ppermute | solution.py:339
  26.9 3.7 %copy-start = (f32[4,3,1024]{2,0,1:T(4,128)S(1)}, f32[4,3,1024]{2,0,1:T(4,128)}, u32[]{:S(2)}) copy-start(f32[4,3,1024]{2,0,1:T(4,128)} %param.4) | copy-start | bytes 147460
  51.0 27.9 %collective-permute-start.5 = (bf16[256,2048]{1,0:T(8,128)(2,1)}, bf16[256,2048]{1,0:T(8,128)(2,1)}, u32[]{:S(2)}, u32[]{:S(2)}) collective-permute-start(bf16[256,2048]{1,0:T(8,128)(2,1)} %get-tuple-element.52), channel_id=1, source_target_pairs={{0,64},{32,96},{64,0},{96,32},{1,65},{33,97},{65,1},{97,33},{2,66}... | collective-permute-start | bytes 3145736 | tf_op jit(solution)/shard_map/ppermute | solution.py:327
  53.9 46.1 %collective-permute-start.9 = (bf16[256,2048]{1,0:T(8,128)(2,1)}, bf16[256,2048]{1,0:T(8,128)(2,1)}, u32[]{:S(2)}, u32[]{:S(2)}) collective-permute-start(bf16[256,2048]{1,0:T(8,128)(2,1)} %get-tuple-element.63), channel_id=1, source_target_pairs={{0,64},{32,96},{64,0},{96,32},{1,65},{33,97},{65,1},{97,33},{2,66}... | collective-permute-start | bytes 3145736 | tf_op jit(solution)/shard_map/ppermute | solution.py:327
  54.6 26.3 %collective-permute-start.10 = (bf16[384,2048]{1,0:T(8,128)(2,1)}, bf16[384,2048]{1,0:T(8,128)(2,1)}, u32[]{:S(2)}, u32[]{:S(2)}) collective-permute-start(bf16[384,2048]{1,0:T(8,128)(2,1)} %collective-permute-done.refs_5_), channel_id=1, source_target_pairs={{1,0},{2,1},{3,2},{4,3},{5,4},{6,5},{7,6},{8,7},{9,8},{10,9},{11,1... | collective-permute-start | bytes 4718600 | tf_op jit(solution)/shard_map/ppermute | solution.py:339
  59.9 24.2 %collective-permute-start.11 = (bf16[384,2048]{1,0:T(8,128)(2,1)}, bf16[384,2048]{1,0:T(8,128)(2,1)}, u32[]{:S(2)}, u32[]{:S(2)}) collective-permute-start(bf16[384,2048]{1,0:T(8,128)(2,1)} %collective-permute-done.6.refs_7_), channel_id=1, source_target_pairs={{0,1},{1,2},{2,3},{3,4},{4,5},{5,6},{6,7},{7,8},{8,9},{9,10},{10,1... | collective-permute-start | bytes 4718600 | tf_op jit(solution)/shard_map/ppermute | solution.py:339
  78.9 23.0 %collective-permute-start.8 = (bf16[256,2048]{1,0:T(8,128)(2,1)}, bf16[256,2048]{1,0:T(8,128)(2,1)}, u32[]{:S(2)}, u32[]{:S(2)}) collective-permute-start(bf16[256,2048]{1,0:T(8,128)(2,1)} %collective-permute-done.5.refs_2_), channel_id=1, source_target_pairs={{0,1},{1,2},{2,3},{3,4},{4,5},{5,6},{6,7},{7,8},{8,9},{9,10},{10,1... | collective-permute-start | bytes 3145736 | tf_op jit(solution)/shard_map/ppermute | solution.py:339
  100.0 18.9 %collective-permute-start.12 = (bf16[256,2048]{1,0:T(8,128)(2,1)}, bf16[256,2048]{1,0:T(8,128)(2,1)}, u32[]{:S(2)}, u32[]{:S(2)}) collective-permute-start(bf16[256,2048]{1,0:T(8,128)(2,1)} %collective-permute-done.9.refs_3_), channel_id=1, source_target_pairs={{0,1},{1,2},{2,3},{3,4},{4,5},{5,6},{6,7},{7,8},{8,9},{9,10},{10,1... | collective-permute-start | bytes 3145736 | tf_op jit(solution)/shard_map/ppermute | solution.py:339
